TPU v7x, 32 devices: a whole 2x2x4 slice. The times are simulated.
32 devices in a mesh: grp: 4 (over y, x), seq: 8 (over z, core).
Axes of the slice: x: 2, y: 2, z: 4, core: 2. Of those that a mesh axis runs over, the one named last changes fastest.
Arguments:
- tokens: bfloat16 [128, 1024], P(('grp', 'seq')), may hold values from -6 to 6
- attn_gain: float32 [1024], replicated, may hold values from 0.1 to 1.9
- w_qkv: bfloat16 [1024, 3072], replicated, may hold values from -0.1875 to 0.1875
- w_out: bfloat16 [1024, 1024], replicated, may hold values from -0.1875 to 0.1875
- mlp_gain: float32 [1024], replicated, may hold values from 0.1 to 1.9
- w_gate_up: bfloat16 [2, 1024, 4096], P(None, None, 'seq'), may hold values from -0.1875 to 0.1875
- w_down: bfloat16 [4096, 1024], P('seq'), may hold values from -0.09375 to 0.09375
- kv_cache: bfloat16 [384, 2, 64, 1024], P(('grp', 'seq'))
- block_owner: int32 [384], P(('grp', 'seq')), may hold values from 0 to 31, as said below
- block_fill: int32 [384], P(('grp', 'seq')), may hold values from 0 to 64, as said below
Outputs:
- output: bfloat16 [128, 1024], P(('grp', 'seq'))
Inputs may be any that keep to these rules, and one draw needn't show every extreme that they name: `block_fill`: each request has at least one block; in each group one request fills exactly 32 whole blocks, every other has at most 2 blocks; blocks of one request are live from their start and all but its last are full; blocks with no live token exist in every group. `block_owner`: every served request number of a group names some block of that group.
All inputs are finite; a program needn't handle non-finite values.
Results may differ from a plain program's by a relative error of at most 0.024.
Values may be sent and summed in bfloat16 or wider, within the bound.
A program may use at most 320 MiB of HBM per device.

v0:
```python
import jax
import jax.numpy as jnp
from jax import lax
from jax.sharding import PartitionSpec as P

HEADS = 16


floor_score = -1e30
epsilon = 1e-05


def rms_scaled(row_data, gain):
    values = row_data.astype(jnp.float32)
    return values * lax.rsqrt(jnp.mean(values * values, axis=-1, keepdims=True) + epsilon) * gain


def body(
    tokens, attn_gain, w_qkv, w_out, mlp_gain, w_gate_up, w_down, kv_cache, block_owner, block_fill
):
    groups = lax.axis_size("grp")
    row_count, feature_count = tokens.shape
    head_count = HEADS
    head_dim = feature_count // head_count
    per_group = row_count // groups
    score_scale = head_dim ** (-0.5)
    normed = rms_scaled(tokens, attn_gain).astype(jnp.bfloat16)
    qkv = jnp.dot(normed, w_qkv, preferred_element_type=jnp.float32).astype(jnp.bfloat16)
    sent_qkv, sent_input = (
        lax.all_to_all(
            qkv.reshape(per_group, groups, 3 * feature_count),
            "grp",
            split_axis=1,
            concat_axis=1,
            tiled=True,
        ),
        lax.all_to_all(
            tokens.reshape(per_group, groups, feature_count),
            "grp",
            split_axis=1,
            concat_axis=1,
            tiled=True,
        ),
    )
    served_qkv = sent_qkv.reshape(row_count, 3 * feature_count)
    served_input = sent_input.reshape(row_count, feature_count)
    query_own = served_qkv[:, :feature_count]
    key_own = served_qkv[:, feature_count : 2 * feature_count]
    value_own = served_qkv[:, 2 * feature_count :]
    offset = lax.axis_index("seq") * row_count
    query_all = lax.all_gather(query_own, "seq", axis=0, tiled=True)
    group_rows = query_all.shape[0]
    blocks, _, span, _ = kv_cache.shape
    key_block = kv_cache[:, 0].reshape(blocks, span, head_count, head_dim)
    value_block = kv_cache[:, 1].reshape(blocks, span, head_count, head_dim)
    query_blocks = query_all[block_owner].reshape(blocks, head_count, head_dim)
    scores = (
        jnp.einsum("bhd,bthd->bht", query_blocks, key_block, preferred_element_type=jnp.float32)
        * score_scale
    )
    is_valid = (
        lax.broadcasted_iota(jnp.int32, (blocks, head_count, span), 2) < block_fill[:, None, None]
    )
    masked = jnp.where(is_valid, scores, floor_score)
    block_max = jnp.max(masked, axis=2)
    weights = jnp.where(is_valid, jnp.exp(masked - block_max[:, :, None]), 0.0).astype(jnp.bfloat16)
    block_total = jnp.sum(weights.astype(jnp.float32), axis=2)
    block_sum = jnp.einsum(
        "bht,bthd->bhd", weights, value_block, preferred_element_type=jnp.float32
    )
    member = block_owner[None, :] == lax.broadcasted_iota(jnp.int32, (group_rows, blocks), 0)
    local_max = jnp.max(jnp.where(member[:, :, None], block_max[None, :, :], floor_score), axis=1)
    factor = jnp.exp(block_max - local_max[block_owner])
    member_table = member.astype(jnp.float32)
    local_total = jnp.dot(member_table, block_total * factor, precision=lax.Precision.HIGHEST)
    local_sum = jnp.dot(
        member_table,
        (block_sum * factor[:, :, None]).reshape(blocks, feature_count),
        precision=lax.Precision.HIGHEST,
    )
    own_max = lax.dynamic_slice_in_dim(local_max, offset, row_count, 0)
    own_total = lax.dynamic_slice_in_dim(local_total, offset, row_count, 0)
    own_sum = lax.dynamic_slice_in_dim(local_sum, offset, row_count, 0)
    query_float = query_own.astype(jnp.float32).reshape(row_count, head_count, head_dim)
    key_float = key_own.astype(jnp.float32).reshape(row_count, head_count, head_dim)
    own_score = jnp.sum(query_float * key_float, axis=2) * score_scale
    joined = jnp.maximum(own_max, own_score)
    keep_weight = jnp.exp(own_max - joined)
    own_weight = jnp.exp(own_score - joined)
    new_total = own_total * keep_weight + own_weight
    new_sum = own_sum.reshape(row_count, head_count, head_dim) * keep_weight[:, :, None]
    new_sum = (
        new_sum
        + value_own.astype(jnp.float32).reshape(row_count, head_count, head_dim)
        * own_weight[:, :, None]
    )
    local_max = lax.dynamic_update_slice_in_dim(local_max, joined, offset, 0)
    local_total = lax.dynamic_update_slice_in_dim(local_total, new_total, offset, 0)
    local_sum = lax.dynamic_update_slice_in_dim(
        local_sum, new_sum.reshape(row_count, feature_count), offset, 0
    )
    local_max, local_total, local_sum = (local_max, local_total, local_sum)
    maxima = lax.pmax(local_max, "seq")
    factor = jnp.exp(local_max - maxima)
    scaled_sum = (
        local_sum.reshape(local_sum.shape[0], head_count, head_dim) * factor[:, :, None]
    ).reshape(local_sum.shape)
    totals, weighted = (
        lax.psum_scatter(local_total * factor, "seq", scatter_dimension=0, tiled=True),
        lax.psum_scatter(scaled_sum, "seq", scatter_dimension=0, tiled=True),
    )
    scaled = weighted.reshape(weighted.shape[0], head_count, head_dim) / totals[:, :, None]
    context = scaled.reshape(weighted.shape[0], feature_count).astype(jnp.bfloat16)
    mixed_rows = served_input.astype(jnp.float32) + jnp.dot(
        context, w_out, preferred_element_type=jnp.float32
    )
    normed_mlp = rms_scaled(mixed_rows, mlp_gain).astype(jnp.bfloat16)
    rows_piece = lax.all_gather(normed_mlp, "seq", axis=0, tiled=True)
    gate_part = jnp.dot(rows_piece, w_gate_up[0], preferred_element_type=jnp.float32)
    up_part = jnp.dot(rows_piece, w_gate_up[1], preferred_element_type=jnp.float32)
    hidden = (jax.nn.silu(gate_part) * up_part).astype(jnp.bfloat16)
    partial_value = jnp.dot(hidden, w_down, preferred_element_type=jnp.float32)
    residual, partial_value = (mixed_rows, partial_value)
    down_sum = lax.psum_scatter(partial_value, "seq", scatter_dimension=0, tiled=True)
    output = (residual + down_sum).astype(jnp.bfloat16)
    returned = lax.all_to_all(
        output.reshape(per_group, groups, feature_count),
        "grp",
        split_axis=1,
        concat_axis=1,
        tiled=True,
    )
    return returned.reshape(row_count, feature_count)


def solution(mesh):
    in_specs = (
        P(("grp", "seq"), None),
        P(),
        P(),
        P(),
        P(),
        P(None, None, "seq"),
        P("seq", None),
        P(("grp", "seq"), None, None, None),
        P(("grp", "seq")),
        P(("grp", "seq")),
    )
    out_specs = P(("grp", "seq"), None)
    return jax.shard_map(body, mesh=mesh, in_specs=in_specs, out_specs=out_specs, check_vma=False)
```

profile of v0, /device:TPU:0, one launch (start us, length us, event | category | flops | bytes accessed | tf_op | source)
XLA Modules:
  0.0 227.3 jit_solution(12327401021514487746)
XLA Ops:
  6.5 0.9 copy.82
  7.9 0.6 reduce.1
  9.1 5.2 %all-to-all-start = ((bf16[4,2,512]{2,1,0:T(2,128)(2,1)}), bf16[4,2,512]{2,1,0:T(2,128)(2,1)S(1)}, u32[]{:S(2)}, u32[]{:S(2)}) async-start(bf16[4,2,512]{2,1,0:T(2,128)(2,1)} %reshape.126), calls=%async_computation | async-start | bytes 16384 | tf_op jit(solution)/shard_map/all_to_all | solution.py:37
  14.3 0.8 fusion.20
  15.1 4.2 %fusion.39 = (bf16[12,1,64,1024]{3,2,1,0:T(8,128)(2,1)}, bf16[12,1,64,1024]{3,2,1,0:T(8,128)(2,1)}) fusion(bf16[12,2,64,1024]{3,2,1,0:T(8,128)(2,1)} %param.17), kind=kLoop, calls=%fused_computation.70 | loop fusion | bytes 6291456 | tf_op jit(solution)/shard_map/slice | solution.py:55
  19.4 1.0 fusion
  20.4 0.7 reduce
  21.1 0.6 reshape.124
  21.8 4.2 %all-to-all-start.1 = ((bf16[4,2,1536]{2,1,0:T(2,128)(2,1)}), bf16[4,2,1536]{2,1,0:T(2,128)(2,1)S(1)}, u32[]{:S(2)}, u32[]{:S(2)}) async-start(bf16[4,2,1536]{2,1,0:T(2,128)(2,1)} %reshape.124), calls=%async_computation.1 | async-start | bytes 49152 | tf_op jit(solution)/shard_map/all_to_all | solution.py:30
  26.0 4.2 %copy.62 = bf16[12,1,64,1024]{2,3,0,1:T(8,128)(2,1)} copy(bf16[12,1,64,1024]{3,2,1,0:T(8,128)(2,1)} %get-tuple-element.14) | data formatting | bytes 3145728 | tf_op jit(solution)/shard_map/reshape;squeeze | solution.py:54
  30.1 5.3 %reshape_squeeze.7 = bf16[12,64,16,64]{3,2,1,0:T(8,128)(2,1)} reshape(bf16[12,1,64,1024]{3,2,1,0:T(8,128)(2,1)} %get-tuple-element.13) | data formatting | bytes 3145728 | tf_op jit(solution)/shard_map/reshape;squeeze | solution.py:55
  36.6 0.6 reshape.127
  37.9 14.2 %all-gather = bf16[8,4,1024]{2,1,0:T(4,128)(2,1)S(1)} all-gather(bf16[1,4,1024]{2,1,0:T(4,128)(2,1)S(1)} %slice_bitcast_fusion), channel_id=1, replica_groups=mesh['grp'=4,'seq'=8] {'seq'}, dimensions={0}, use_global_device_ids=true | all-gather | bytes 73728 | tf_op jit(solution)/shard_map/all_gather | solution.py:51
  52.8 2.8 %fusion.40 = f32[12,16,1,64]{3,2,1,0:T(1,128)S(1)} fusion(bf16[12,16,64,1]{2,3,1,0:T(2,128)(2,1)S(1)} %reshape.118, bf16[12,64,16,64]{1,3,2,0:T(8,128)(2,1)} %bitcast.56), kind=kOutput, calls=%fused_computation.74 | convolution fusion | flops 1572864 | bytes 1646592 | tf_op jit(solution)/shard_map/bhd,bthd->bht/dot_general | solution.py:58
  57.4 0.7 mul.131
  58.2 0.7 mul.134
  58.8 2.8 %fusion.1 = f32[12,16,1,64]{3,2,1,0:T(1,128)S(1)} fusion(bf16[12,64,16,64]{3,2,1,0:T(8,128)(2,1)} %reshape_squeeze.7, bf16[12,16,64,1]{2,1,0,3:T(8,128)(2,1)S(1)} %bitcast.69), kind=kOutput, calls=%fused_computation.4 | convolution fusion | flops 1572864 | bytes 1646592 | tf_op jit(solution)/shard_map/bht,bthd->bhd/dot_general | solution.py:68
  62.7 17.2 %pmax.7 = f32[32,16]{0,1:T(8,128)S(1)} all-reduce(f32[32,16]{0,1:T(8,128)S(1)} %dynamic_update_slice.10), channel_id=1, replica_groups=mesh['grp'=4,'seq'=8] {'seq'}, use_global_device_ids=true, to_apply=%region_4.5 | all-reduce | flops 512 | bytes 4096 | tf_op jit(solution)/shard_map/pmax | solution.py:103
  79.9 0.6 fusion.38
  80.7 0.8 mul.137
  81.5 0.8 add_dynamic-update-slice_fusion
  82.3 1.6 mul.138
  83.9 14.1 %all-reduce.1 = f32[32,16]{0,1:T(8,128)S(1)} all-reduce(f32[32,16]{0,1:T(8,128)} %get-tuple-element.5), channel_id=3, replica_groups=mesh['grp'=4,'seq'=8] {'seq'}, use_global_device_ids=true, to_apply=%region_7.8.clone | all-reduce | flops 512 | bytes 4096
  98.3 38.6 %all-reduce.6.cloned.1.call-done = f32[32,1024]{1,0:T(8,128)} async-done(((f32[32,1024]{1,0:T(8,128)}), f32[32,1024]{1,0:T(8,128)}) %all-reduce.6.cloned.1.call-update) | async-done | bytes 131088
  136.9 1.3 multiply_reduce_fusion
  138.2 0.8 fusion.26
  139.0 14.0 %all-gather.1 = bf16[8,4,1024]{2,1,0:T(4,128)(2,1)S(1)} all-gather(bf16[1,4,1024]{2,1,0:T(4,128)(2,1)S(1)} %fusion.26), channel_id=1, replica_groups=mesh['grp'=4,'seq'=8] {'seq'}, dimensions={0}, use_global_device_ids=true | all-gather | bytes 73728 | tf_op jit(solution)/shard_map/all_gather | solution.py:118
  152.9 1.5 fusion.7
  154.4 2.4 %fusion.4 = f32[32,1024]{1,0:T(8,128)} fusion(bf16[512,1024]{1,0:T(8,128)(2,1)S(1)} %copy-done.2, bf16[32,1024]{1,0:T(8,128)(2,1)S(1)} %reshape.112, bf16[2,1024,512]{2,1,0:T(8,128)(2,1)} %param.15, f32[32,512]{1,0:T(8,128)S(1)} %fusion.7), kind=kOutput, calls=%fused_computation.8 | convolution fusion | flops 67207168 | bytes 2359296 | tf_op jit(solution)/shard_map/dot_general | solution.py:122
  156.9 53.3 %all-reduce.8.cloned.1.call-done = f32[32,1024]{1,0:T(8,128)} async-done(((f32[32,1024]{1,0:T(8,128)}), f32[32,1024]{1,0:T(8,128)}) %all-reduce.8.cloned.1.call-update) | async-done | bytes 131088
  210.2 0.8 fusion.27
  211.7 8.1 %all_to_all.15 = bf16[4,2,512]{2,1,0:T(2,128)(2,1)S(1)} all-to-all(bf16[4,2,512]{2,1,0:T(2,128)(2,1)S(1)} %reshape.128), channel_id=1, replica_groups=mesh['grp'=4,'seq'=8] {'grp'}, dimensions={0} | all-to-all | bytes 16384 | tf_op jit(solution)/shard_map/all_to_all | solution.py:126
  (73 shorter events, 7.8 us)
Async XLA Ops:
  6.5 130.4 %copy-start = (bf16[1024,1024]{1,0:T(8,128)(2,1)S(1)}, bf16[1024,1024]{1,0:T(8,128)(2,1)}, u32[]{:S(2)}) copy-start(bf16[1024,1024]{1,0:T(8,128)(2,1)} %param.13) | copy-start | bytes 6291460
  7.9 11.5 %copy-start.7 = (s32[12]{0:T(128)S(1)}, s32[12]{0:T(128)}, u32[]{:S(2)}) copy-start(s32[12]{0:T(128)} %param.18) | copy-start | bytes 148
  7.9 11.5 %copy-start.4 = (bf16[4,1024]{1,0:T(4,128)(2,1)S(1)}, bf16[4,1024]{1,0:T(4,128)(2,1)}, u32[]{:S(2)}) copy-start(bf16[4,1024]{1,0:T(4,128)(2,1)} %param.10) | copy-start | bytes 24580
  7.9 11.5 %copy-start.5 = (f32[1024]{0:T(1024)S(1)}, f32[1024]{0:T(1024)}, u32[]{:S(2)}) copy-start(f32[1024]{0:T(1024)} %param.11) | copy-start | bytes 12292
  9.1 12.6 %all-to-all-start = ((bf16[4,2,512]{2,1,0:T(2,128)(2,1)}), bf16[4,2,512]{2,1,0:T(2,128)(2,1)S(1)}, u32[]{:S(2)}, u32[]{:S(2)}) async-start(bf16[4,2,512]{2,1,0:T(2,128)(2,1)} %reshape.126), calls=%async_computation | async-start | bytes 16384 | tf_op jit(solution)/shard_map/all_to_all | solution.py:37
  15.1 4.3 %copy-start.1 = (bf16[1024,3072]{1,0:T(8,128)(2,1)S(1)}, bf16[1024,3072]{1,0:T(8,128)(2,1)}, u32[]{:S(2)}) copy-start(bf16[1024,3072]{1,0:T(8,128)(2,1)} %param.12) | copy-start | bytes 18874372
  21.8 15.5 %all-to-all-start.1 = ((bf16[4,2,1536]{2,1,0:T(2,128)(2,1)}), bf16[4,2,1536]{2,1,0:T(2,128)(2,1)S(1)}, u32[]{:S(2)}, u32[]{:S(2)}) async-start(bf16[4,2,1536]{2,1,0:T(2,128)(2,1)} %reshape.124), calls=%async_computation.1 | async-start | bytes 49152 | tf_op jit(solution)/shard_map/all_to_all | solution.py:30
  25.9 111.0 %all-reduce.6.cloned.1.call-start = ((), (), s32[]{:S(2)}) async-start(), calls=%async_computation.3 | async-start | bytes 262144
  30.1 5.3 %copy-start.8 = (u32[32]{0:T(128)S(1)}, u32[32]{0:T(128)}, u32[]{:S(2)}) copy-start(u32[32]{0:T(128)} %constant.36) | copy-start | bytes 388
  35.4 20.2 %copy-start.6 = (s32[12]{0:T(128)S(1)}, s32[12]{0:T(128)}, u32[]{:S(2)}) copy-start(s32[12]{0:T(128)} %param.19) | copy-start | bytes 148
  37.3 0.6 copy-start.3
  61.7 92.8 %copy-start.2 = (bf16[512,1024]{1,0:T(8,128)(2,1)S(1)}, bf16[512,1024]{1,0:T(8,128)(2,1)}, u32[]{:S(2)}) copy-start(bf16[512,1024]{1,0:T(8,128)(2,1)} %param.16) | copy-start | bytes 3145732
  83.8 126.4 %all-reduce.8.cloned.1.call-start = ((), (), s32[]{:S(2)}) async-start(), calls=%async_computation.4 | async-start | bytes 262144
Sparse Core Ops, SparseCore 0:
  84.0 52.9 all-reduce.5
  157.0 53.1 all-reduce.7
where the time goes:
time: 228 us; the launch traced here: 227 us
  waiting for transfers between devices  92 us (40%)
  blocking collectives  67.6 us (30%)
  local copies, waits for them, and re-layouts  23.7 us (10%)
  between operations  14.3 us (6%)
  matrix products  12.3 us (5%)
  starting transfers between devices  9.4 us (4%)
  other arithmetic  7.97 us (3%)
    unnamed x4, waiting for transfers between devices  92 us
    pmax x1, blocking collectives, body(): maxima = lax.pmax(local_max, 'seq')  17.2 us
    all_gather x1, blocking collectives, body(): query_all = lax.all_gather(query_own, 'seq', axis=0, tiled=True)  14.2 us
    unnamed x1, blocking collectives  14.1 us
    all_gather x1, blocking collectives, body(): rows_piece = lax.all_gather(normed_mlp, 'seq', axis=0, tiled=True)  14 us
    all_to_all x1, blocking collectives, body(): lax.all_to_all(output.reshape(per_group, groups, feature_count), 'grp', s...  8.14 us
    another operation x1, local copies, waits for them, and re-layouts, body(): value_block = kv_cache[:, 1].reshape(blocks, span, head_count, head_dim)  5.27 us
    all_to_all x1, starting transfers between devices, body(): lax.all_to_all(tokens.reshape(per_group, groups, feature_count), 'grp', s...  5.16 us
  transfers between devices with their start and end apart: 4, of which 2 were waited for; matrix products, arithmetic and copies ran while one was open for 8% of the time, Pallas kernels for 0%

commit v1 on v0

v1 whole, which is shorter than its diff:
```python
import functools

import jax
import jax.numpy as jnp
from jax import lax
from jax.experimental import pallas as pl
from jax.experimental.pallas import tpu as pltpu
from jax.sharding import PartitionSpec as P

HEADS = 16
floor_score = -1e30
epsilon = 1e-05
MESH = pl.DeviceIdType.MESH
f32 = jnp.float32
bf16 = jnp.bfloat16


def iota(shape, dim):
    return lax.broadcasted_iota(jnp.int32, shape, dim)


def kernel(
    groups, shards,
    tokens, attn_gain, w_qkv, w_out, mlp_gain, w_gate_up, w_down, kv_cache, owner, fill,
    out_ref,
    wq, wkv, wo, wgu, wd, kc, vc,
    tok_rows, tok_all, stat_out, stat_in, part, merged, rows_all, lhs, down, home, total,
    load_sem, send_sem, recv_sem,
):
    g = lax.axis_index("grp")
    s = lax.axis_index("seq")
    width = tokens.shape[1]
    head_dim = width // HEADS
    quarter = width // 4
    chunks = width // 128
    devices = groups * shards
    rows = groups * shards
    blocks, _, span, _ = kv_cache.shape
    lanes = 256
    scale = head_dim ** (-0.5)

    loads = [
        pltpu.make_async_copy(w_qkv.at[:, pl.ds(0, width)], wq, load_sem.at[0]),
        pltpu.make_async_copy(kv_cache.at[:, 0], kc, load_sem.at[1]),
        pltpu.make_async_copy(kv_cache.at[:, 1], vc, load_sem.at[2]),
        pltpu.make_async_copy(w_qkv.at[:, pl.ds(width, 2 * width)], wkv, load_sem.at[3]),
        pltpu.make_async_copy(w_out, wo, load_sem.at[4]),
        pltpu.make_async_copy(w_gate_up, wgu, load_sem.at[5]),
        pltpu.make_async_copy(w_down, wd, load_sem.at[6]),
    ]

    barrier = pltpu.get_barrier_semaphore()

    to_groups = [g] + [lax.rem(g + i, groups) for i in range(1, groups)]

    def each_device(act):
        def at(step, carry):
            to_shard = lax.rem(s + step, shards)
            for to_group in to_groups:
                act(to_group, to_shard)
            return carry

        lax.fori_loop(1, shards, at, 0)
        for to_group in to_groups[1:]:
            act(to_group, s)

    def each_shard(act):
        if shards <= 8:
            for step in range(1, shards):
                act(lax.rem(s + step, shards))
            return

        def at(step, carry):
            act(lax.rem(s + step, shards))
            return carry

        lax.fori_loop(1, shards, at, 0)

    def greet(to_group, to_shard):
        pl.semaphore_signal(
            barrier, inc=1, device_id=(to_group, to_shard), device_id_type=MESH
        )

    each_device(greet)
    for load in loads:
        load.start()
    mine = tokens[...].astype(f32)
    for k in range(chunks):
        tok_rows[pl.ds(k, groups, stride=chunks), :] = mine[:, 128 * k : 128 * (k + 1)]
    pl.semaphore_wait(barrier, devices - 1)

    def tile(index):
        return pl.ds(pl.multiple_of(index * chunks, chunks), chunks)

    def drain(ref, sem):
        pltpu.make_async_copy(ref, ref, sem).wait()

    def send_token(to_group, to_shard):
        pltpu.make_async_remote_copy(
            src_ref=tok_rows.at[tile(to_group)],
            dst_ref=tok_all.at[tile(s * groups + g)],
            send_sem=send_sem.at[0], recv_sem=recv_sem.at[0],
            device_id=(to_group, to_shard), device_id_type=MESH,
        ).start()

    each_device(send_token)
    tok_all[tile(s * groups + g), :] = tok_rows[tile(g), :]

    lane_block = lax.div(iota((1, lanes), 1), HEADS)
    lane_owner = jnp.full((1, lanes), -1, jnp.int32)
    lane_fill = jnp.zeros((1, lanes), jnp.int32)
    for b in range(blocks):
        lane_owner = jnp.where(lane_block == b, owner[b], lane_owner)
        lane_fill = jnp.where(lane_block == b, fill[b], lane_fill)
    pick = jnp.concatenate(
        [(iota((HEADS, rows), 1) == owner[b]).astype(f32) for b in range(blocks)]
        + [jnp.zeros((lanes - blocks * HEADS, rows), f32)], axis=0,
    ).astype(bf16)
    member = iota((rows, lanes), 0) == lane_owner
    head_mask = lax.div(iota((HEADS, width), 1), head_dim) == iota((HEADS, width), 0)

    everyone = tok_all.at[pl.ds(0, (devices - 1) * chunks)]
    drain(everyone, recv_sem.at[0])
    x = jnp.concatenate(
        [tok_all[pl.ds(k, rows, stride=chunks), :] for k in range(chunks)], axis=1
    )
    normed = (
        x * lax.rsqrt(jnp.mean(x * x, axis=-1, keepdims=True) + epsilon) * attn_gain[...]
    ).astype(bf16)
    loads[0].wait()
    query = jnp.dot(normed, wq[...], preferred_element_type=f32).astype(bf16)

    spread = jnp.dot(pick, query, preferred_element_type=f32)
    query_heads = jnp.concatenate(
        [
            jnp.where(head_mask, spread[HEADS * b : HEADS * (b + 1)], 0.0)
            for b in range(lanes // HEADS)
        ], axis=0,
    ).astype(bf16)
    loads[1].wait()
    crossed = lax.dot_general(
        kc[...].reshape(blocks * span, width), query_heads,
        (((1,), (1,)), ((), ())), preferred_element_type=f32,
    )
    scores = jnp.zeros((span, lanes), f32)
    for b in range(blocks):
        scores = jnp.where(lane_block == b, crossed[span * b : span * (b + 1)], scores)
    valid = iota((span, lanes), 0) < lane_fill
    masked = jnp.where(valid, scores * scale, floor_score)
    block_max = jnp.max(masked, axis=0, keepdims=True)
    local_max = jnp.where(member, block_max, floor_score)
    for shift in (16, 32, 64, 128):
        local_max = jnp.maximum(local_max, pltpu.roll(local_max, shift, 1))
    shared_max = jnp.max(jnp.where(member, local_max, floor_score), axis=0, keepdims=True)
    weights = jnp.where(valid, jnp.exp(masked - shared_max), 0.0)
    weights = weights.astype(bf16).astype(f32)
    local_total = jnp.where(member, jnp.sum(weights, axis=0, keepdims=True), 0.0)
    for shift in (16, 32, 64, 128):
        local_total = local_total + pltpu.roll(local_total, shift, 1)
    lane = iota((rows, 128), 1)
    stats = jnp.where(
        lane < HEADS, local_max[:, :128], jnp.where(lane < 2 * HEADS, local_total[:, :128], 0.0)
    )
    stat_low = iota((8, 128), 0) < 4
    for i in range(rows // 8):
        stat = stats[8 * i : 8 * i + 8]
        turned = pltpu.roll(stat, 4, 0)
        stat_out[2 * i] = jnp.where(stat_low, stat, turned)
        stat_out[2 * i + 1] = jnp.where(stat_low, turned, stat)

    def send_stat(to_shard):
        pltpu.make_async_remote_copy(
            src_ref=stat_out.at[to_shard], dst_ref=stat_in.at[s],
            send_sem=send_sem.at[4], recv_sem=recv_sem.at[4],
            device_id=(g, to_shard), device_id_type=MESH,
        ).start()

    each_shard(send_stat)
    stat_in[s] = stat_out[s]

    stacked = jnp.concatenate(
        [jnp.where(lax.rem(lane_block, 4) == j, weights, 0.0) for j in range(4)], axis=0
    )
    stacked = jnp.transpose(stacked).astype(bf16)
    loads[2].wait()
    products = []
    for i in range(blocks // 4):
        product = jnp.dot(
            stacked[4 * HEADS * i : 4 * HEADS * (i + 1)],
            vc[4 * i : 4 * i + 4].reshape(4 * span, width), preferred_element_type=f32,
        )
        for j in range(4):
            products.append(jnp.where(head_mask, product[HEADS * j : HEADS * (j + 1)], 0.0))
    products.append(jnp.zeros((lanes - blocks * HEADS, width), f32))
    local_sum = jnp.dot(
        member.astype(f32).astype(bf16), jnp.concatenate(products, axis=0).astype(bf16),
        preferred_element_type=f32,
    )

    is_low = iota((8, quarter), 0) < 4
    for i in range(rows // 8):
        q = [
            local_sum[8 * i : 8 * i + 8, quarter * c : quarter * (c + 1)] for c in range(4)
        ]
        for c in (0, 2):
            even = jnp.where(is_low, q[c], pltpu.roll(q[c + 1], 4, 0))
            odd = jnp.where(is_low, pltpu.roll(q[c], 4, 0), q[c + 1])
            q[c], q[c + 1] = even, odd
        part[2 * i] = jnp.concatenate([q[0], q[2]], axis=0).astype(bf16)
        part[2 * i + 1] = jnp.concatenate([q[1], q[3]], axis=0).astype(bf16)

    def send_part(to_shard):
        pltpu.make_async_remote_copy(
            src_ref=part.at[to_shard], dst_ref=merged.at[s],
            send_sem=send_sem.at[1], recv_sem=recv_sem.at[1],
            device_id=(g, to_shard), device_id_type=MESH,
        ).start()

    each_shard(send_part)
    merged[s] = part[s]

    own_rows = (iota((8, rows), 1) == s * groups + lax.rem(iota((8, rows), 0), 4)).astype(f32)
    own_rows = own_rows.astype(bf16)
    own_query = jnp.dot(own_rows, query, preferred_element_type=f32)
    own_normed = jnp.dot(own_rows, normed, preferred_element_type=f32).astype(bf16)
    own_tokens = jnp.dot(own_rows, x.astype(bf16), preferred_element_type=f32)
    loads[3].wait()
    own_kv = jnp.dot(own_normed, wkv[...], preferred_element_type=f32).astype(bf16).astype(f32)
    own_key, own_value = own_kv[:, :width], own_kv[:, width:]
    fold = (lax.div(iota((width, 128), 0), head_dim) == iota((width, 128), 1)).astype(f32)
    own_score = (
        jnp.dot(
            own_query * own_key, fold,
            precision=lax.Precision.HIGHEST, preferred_element_type=f32,
        ) * scale
    )
    value = [own_value[:, quarter * c : quarter * (c + 1)] for c in range(4)]
    own_value = jnp.concatenate(
        [jnp.where(is_low, value[0], value[1]), jnp.where(is_low, value[2], value[3])], axis=0
    )
    expand_head = lax.rem(iota((256, quarter), 0), 128)
    expand = (
        (expand_head < HEADS)
        & (lax.rem(expand_head, HEADS // 4) == lax.div(iota((256, quarter), 1), head_dim))
    ).astype(f32).astype(bf16)
    live = iota((8, 128), 1) < HEADS
    spot = iota((16, 128), 1)
    quarter_heads = (spot < HEADS) & (
        lax.div(spot, HEADS // 4) == lax.div(iota((16, 128), 0), 4)
    )

    drain(stat_in.at[pl.ds(0, shards - 1)], recv_sem.at[4])
    peak = own_score
    for i in range(shards):
        peak = jnp.maximum(peak, stat_in[i])
    own_weight = jnp.exp(own_score - peak)
    factors = []
    totals = own_weight
    for i in range(shards):
        stat = stat_in[i]
        factor = jnp.exp(stat - peak)
        totals = totals + factor * pltpu.roll(stat, 128 - HEADS, 1)
        factors.append(factor)
    factors.append(own_weight)
    inverse = 1.0 / jnp.where(live, totals, 1.0)
    gains = []
    for factor in factors:
        gain = factor * inverse
        gains.append(jnp.where(quarter_heads, jnp.concatenate([gain, gain], axis=0), 0.0))
    gains = jnp.concatenate(gains, axis=0)
    gains_high = gains.astype(bf16)
    gains_low = (gains - gains_high.astype(f32)).astype(bf16)
    gains = jnp.dot(
        jnp.concatenate([gains_high, gains_low], axis=1), expand, preferred_element_type=f32
    )
    context = own_value * gains[16 * shards :]
    loads[4].wait()
    drain(merged.at[pl.ds(0, shards - 1)], recv_sem.at[1])
    for i in range(shards):
        context = context + merged[i].astype(f32) * gains[16 * i : 16 * i + 16]
    context = context.astype(bf16)

    mixed_parts = [
        jnp.dot(
            context, wo[quarter * c : quarter * (c + 1), :], preferred_element_type=f32
        )[8 * (c // 2) : 8 * (c // 2) + 8]
        for c in range(4)
    ]
    mixed_low = mixed_parts[0] + mixed_parts[2]
    mixed_high = mixed_parts[1] + mixed_parts[3]
    mixed = mixed_low + pltpu.roll(mixed_high, 4, 0)
    mixed = own_tokens + jnp.where(iota((8, width), 0) < 4, mixed, pltpu.roll(mixed, 4, 0))
    normed_mlp = (
        mixed * lax.rsqrt(jnp.mean(mixed * mixed, axis=-1, keepdims=True) + epsilon)
        * mlp_gain[...]
    )
    value = [normed_mlp[:, quarter * c : quarter * (c + 1)] for c in range(4)]
    rows_all[s] = jnp.concatenate(
        [jnp.where(is_low, value[0], value[1]), jnp.where(is_low, value[2], value[3])], axis=0
    ).astype(bf16)

    def send_rows(to_shard):
        pltpu.make_async_remote_copy(
            src_ref=rows_all.at[s], dst_ref=rows_all.at[s],
            send_sem=send_sem.at[2], recv_sem=recv_sem.at[2],
            device_id=(g, to_shard), device_id_type=MESH,
        ).start()

    each_shard(send_rows)
    loads[5].wait()
    loads[6].wait()
    drain(rows_all.at[pl.ds(0, shards - 1)], recv_sem.at[2])
    for i in range(rows // 8):
        even, odd = rows_all[2 * i].astype(f32), rows_all[2 * i + 1].astype(f32)
        for c in (0, 2):
            first, second = even[4 * c : 4 * c + 8], odd[4 * c : 4 * c + 8]
            lhs[8 * i : 8 * i + 8, quarter * c : quarter * (c + 1)] = jnp.where(
                is_low, first, pltpu.roll(second, 4, 0)
            )
            lhs[8 * i : 8 * i + 8, quarter * (c + 1) : quarter * (c + 2)] = jnp.where(
                is_low, pltpu.roll(first, 4, 0), second
            )
    mlp_rows = lhs[...].astype(bf16)
    gate = jnp.dot(mlp_rows, wgu[0], preferred_element_type=f32)
    up = jnp.dot(mlp_rows, wgu[1], preferred_element_type=f32)
    hidden = (gate / (1.0 + jnp.exp(-gate)) * up).astype(bf16)
    partial = jnp.dot(hidden, wd[...], preferred_element_type=f32)
    residual = jnp.concatenate([mixed] * (rows // 8), axis=0)
    row_id = iota((rows, width), 0)
    partial = partial + jnp.where(lax.div(row_id, groups) == s, residual, 0.0)
    for k in range(chunks):
        down[pl.ds(k, rows, stride=chunks), :] = partial[:, 128 * k : 128 * (k + 1)]

    def send_down(to_group, to_shard):
        pltpu.make_async_remote_copy(
            src_ref=down.at[tile(to_shard * groups + to_group)],
            dst_ref=home.at[tile(g * shards + s)],
            send_sem=send_sem.at[3], recv_sem=recv_sem.at[3],
            device_id=(to_group, to_shard), device_id_type=MESH,
        ).start()

    each_device(send_down)
    home[tile(g * shards + s), :] = down[tile(s * groups + g), :]
    drain(everyone, send_sem.at[0])
    drain(stat_in.at[pl.ds(0, shards - 1)], send_sem.at[4])
    drain(merged.at[pl.ds(0, shards - 1)], send_sem.at[1])
    drain(rows_all.at[pl.ds(0, shards - 1)], send_sem.at[2])
    drain(home.at[pl.ds(0, (devices - 1) * chunks)], recv_sem.at[3])
    for j in range(groups):
        row = home[j * shards * chunks : (j * shards + 1) * chunks, :]
        for i in range(1, shards):
            at = (j * shards + i) * chunks
            row = row + home[at : at + chunks, :]
        total[j * chunks : (j + 1) * chunks, :] = row
    out_ref[...] = jnp.concatenate(
        [total[pl.ds(k, groups, stride=chunks), :] for k in range(chunks)], axis=1
    )
    drain(home.at[pl.ds(0, (devices - 1) * chunks)], send_sem.at[3])


def body(
    tokens, attn_gain, w_qkv, w_out, mlp_gain, w_gate_up, w_down, kv_cache, block_owner, block_fill
):
    groups, shards = lax.axis_size("grp"), lax.axis_size("seq")
    row_count, width = tokens.shape
    blocks, _, span, _ = kv_cache.shape
    rows = groups * shards
    chunks = width // 128
    assert row_count == groups and chunks == 8 and groups == 4 and blocks % 4 == 0
    vmem = pl.BlockSpec(memory_space=pltpu.VMEM)
    smem = pl.BlockSpec(memory_space=pltpu.SMEM)
    hbm = pl.BlockSpec(memory_space=pl.ANY)
    output = pl.pallas_call(
        functools.partial(kernel, groups, shards),
        out_shape=jax.ShapeDtypeStruct((row_count, width), f32),
        in_specs=[vmem, vmem, hbm, hbm, vmem, hbm, hbm, hbm, smem, smem],
        out_specs=vmem,
        scratch_shapes=[
            pltpu.VMEM((width, width), bf16),
            pltpu.VMEM((width, 2 * width), bf16),
            pltpu.VMEM(w_out.shape, bf16),
            pltpu.VMEM(w_gate_up.shape, bf16),
            pltpu.VMEM(w_down.shape, bf16),
            pltpu.VMEM((blocks, span, width), bf16),
            pltpu.VMEM((blocks, span, width), bf16),
            pltpu.VMEM((row_count * chunks, 128), f32),
            pltpu.VMEM((rows * chunks, 128), f32),
            pltpu.VMEM((shards, 8, 128), f32),
            pltpu.VMEM((shards, 8, 128), f32),
            pltpu.VMEM((shards, 16, width // 4), bf16),
            pltpu.VMEM((shards, 16, width // 4), bf16),
            pltpu.VMEM((shards, 16, width // 4), bf16),
            pltpu.VMEM((rows, width), f32),
            pltpu.VMEM((rows * chunks, 128), f32),
            pltpu.VMEM((rows * chunks, 128), f32),
            pltpu.VMEM((row_count * chunks, 128), f32),
            pltpu.SemaphoreType.DMA((7,)),
            pltpu.SemaphoreType.DMA((5,)),
            pltpu.SemaphoreType.DMA((5,)),
        ],
        compiler_params=pltpu.CompilerParams(
            collective_id=0, has_side_effects=True, vmem_limit_bytes=56 * 2**20
        ),
    )(
        tokens, attn_gain.reshape(1, width), w_qkv, w_out, mlp_gain.reshape(1, width),
        w_gate_up, w_down, kv_cache, block_owner, block_fill,
    )
    return output.astype(bf16)


def solution(mesh):
    in_specs = (
        P(("grp", "seq"), None),
        P(),
        P(),
        P(),
        P(),
        P(None, None, "seq"),
        P("seq", None),
        P(("grp", "seq"), None, None, None),
        P(("grp", "seq")),
        P(("grp", "seq")),
    )
    out_specs = P(("grp", "seq"), None)
    return jax.shard_map(body, mesh=mesh, in_specs=in_specs, out_specs=out_specs, check_vma=False)
```

time: 228 us -> 32.2 us (0.14)
  waiting for transfers between devices: 92 us -> 0 us
  blocking collectives: 67.6 us -> 0 us
  Pallas kernels: 0 us -> 30.6 us
  local copies, waits for them, and re-layouts: 23.7 us -> 0 us
  between operations: 14.3 us -> 0.01 us
  matrix products: 12.3 us -> 0 us
  starting transfers between devices: 9.4 us -> 0 us
  other arithmetic: 7.97 us -> 1.32 us
    unnamed x4 -> x0, waiting for transfers between devices: 92 us -> none
    pallas_call x0 -> x1, Pallas kernels: none -> 30.6 us  [body(): pl.pallas_call(functools.partial(kernel, groups, shards), out_shape=jax.S...]
    all_gather x2 -> x0, blocking collectives: 28.1 us -> none  [the longest x1 14.2 us: body(): query_all = lax.all_gather(query_own, 'seq', axis=0, tiled=True)]
    pmax x1 -> x0, blocking collectives: 17.2 us -> none  [body(): maxima = lax.pmax(local_max, 'seq')]
    unnamed x1 -> x0, blocking collectives: 14.1 us -> none
    dot_general x8 -> x0, matrix products: 12.3 us -> none  [the longest x1 2.82 us: body(): jnp.einsum('bht,bthd->bhd', weights, value_block, preferred_element_type=...]
    another operation x2 -> x0, local copies, waits for them, and re-layouts: 9.42 us -> none  [the longest x1 5.27 us: body(): value_block = kv_cache[:, 1].reshape(blocks, span, head_count, head_dim)]
    all_to_all x2 -> x0, starting transfers between devices: 9.36 us -> none  [the longest x1 5.16 us: body(): lax.all_to_all(tokens.reshape(per_group, groups, feature_count), 'grp', s...]
  transfers between devices with their start and end apart: 4 -> 0, of which waited for: 2 -> 0; matrix products, arithmetic and copies ran while one was open for 8% -> 0% of each run, Pallas kernels for 0% -> 0%
where the time goes in v1:
time: 32.2 us; the launch traced here: 32 us
  Pallas kernels  30.6 us (95%)
  other arithmetic  1.32 us (4%)
    pallas_call x1, Pallas kernels, body(): pl.pallas_call(functools.partial(kernel, groups, shards), out_shape=jax.S...  30.6 us
    convert_element_type x1, other arithmetic, body(): return output.astype(bf16)  1.32 us

profile of v1, /device:TPU:0, one launch (start us, length us, event | category | flops | bytes accessed | tf_op | source)
XLA Modules:
  0.0 32.0 jit_solution(1688031398147168878)
XLA Ops:
  0.0 30.6 %shard_map.100 = f32[4,1024]{1,0:T(4,128)} custom-call(bf16[4,1024]{1,0:T(4,128)(2,1)} %tokens.1, f32[1,1024]{1,0:T(1,128)} %bitcast.2, bf16[1024,3072]{1,0:T(8,128)(2,1)} %w_qkv.1, bf16[1024,1024]{1,0:T(8,128)(2,1)} %w_out.1, f32[1,1024]{1,0:T(1,128)} %bitcast.3, bf16[2,1024,512]{2,1,0:T(8,128)(2,1)} %w_gate_up.1, bf16[512,1024]{1,0:T(8,128)(2,1)} %w_down.1, ...), custom_call_target="tpu_custom_call" | custom-call | tf_op jit(solution)/shard_map/pallas_call | solution.py:373
  30.6 1.3 %convert_element_type.3 = bf16[4,1024]{1,0:T(4,128)(2,1)} convert(f32[4,1024]{1,0:T(4,128)} %shard_map.100) | non-fusion elementwise | flops 4096 | bytes 24576 | tf_op jit(solution)/shard_map/convert_element_type | solution.py:408

commit v2 on v1

v2 whole, which is shorter than its diff:
```python
import functools

import jax
import jax.numpy as jnp
from jax import lax
from jax.experimental import pallas as pl
from jax.experimental.pallas import tpu as pltpu
from jax.sharding import PartitionSpec as P

HEADS = 16
floor_score = -1e30
epsilon = 1e-05
MESH = pl.DeviceIdType.MESH
f32 = jnp.float32
bf16 = jnp.bfloat16


def iota(shape, dim):
    return lax.broadcasted_iota(jnp.int32, shape, dim)


def kernel(
    groups, shards,
    tokens, attn_gain, w_qkv, w_out, mlp_gain, w_gate_up, w_down, kv_cache, owner, fill,
    out_ref,
    wq, wkv, wo, wgu, wd, kc, vc,
    tok_rows, tok_all, stat_all, staged, block_all, unpacked, down, home, total,
    load_sem, send_sem, recv_sem,
):
    g = lax.axis_index("grp")
    s = lax.axis_index("seq")
    width = tokens.shape[1]
    head_dim = width // HEADS
    sums = shards * kv_cache.shape[0]
    padded = -(-sums // 128) * 128
    chunks = width // 128
    devices = groups * shards
    rows = groups * shards
    blocks, _, span, _ = kv_cache.shape
    lanes = 256
    scale = head_dim ** (-0.5)

    loads = [
        pltpu.make_async_copy(w_qkv.at[:, pl.ds(0, width)], wq, load_sem.at[0]),
        pltpu.make_async_copy(kv_cache.at[:, 0], kc, load_sem.at[1]),
        pltpu.make_async_copy(kv_cache.at[:, 1], vc, load_sem.at[2]),
        pltpu.make_async_copy(w_qkv.at[:, pl.ds(width, 2 * width)], wkv, load_sem.at[3]),
        pltpu.make_async_copy(w_out, wo, load_sem.at[4]),
        pltpu.make_async_copy(w_gate_up, wgu, load_sem.at[5]),
        pltpu.make_async_copy(w_down, wd, load_sem.at[6]),
    ]

    barrier = pltpu.get_barrier_semaphore()

    to_groups = [g] + [lax.rem(g + i, groups) for i in range(1, groups)]

    def each_device(act):
        def at(step, carry):
            to_shard = lax.rem(s + step, shards)
            for to_group in to_groups:
                act(to_group, to_shard)
            return carry

        lax.fori_loop(1, shards, at, 0)
        for to_group in to_groups[1:]:
            act(to_group, s)

    def each_shard(act):
        if shards <= 8:
            for step in range(1, shards):
                act(lax.rem(s + step, shards))
            return

        def at(step, carry):
            act(lax.rem(s + step, shards))
            return carry

        lax.fori_loop(1, shards, at, 0)

    def greet(to_group, to_shard):
        pl.semaphore_signal(
            barrier, inc=1, device_id=(to_group, to_shard), device_id_type=MESH
        )

    each_device(greet)
    for load in loads[:3]:
        load.start()
    mine = tokens[...].astype(f32)
    for k in range(chunks):
        tok_rows[pl.ds(k, groups, stride=chunks), :] = mine[:, 128 * k : 128 * (k + 1)]
    pl.semaphore_wait(barrier, devices - 1)

    def tile(index):
        return pl.ds(pl.multiple_of(index * chunks, chunks), chunks)

    def drain(ref, sem):
        pltpu.make_async_copy(ref, ref, sem).wait()

    def send_token(to_group, to_shard):
        pltpu.make_async_remote_copy(
            src_ref=tok_rows.at[tile(to_group)],
            dst_ref=tok_all.at[tile(s * groups + g)],
            send_sem=send_sem.at[0], recv_sem=recv_sem.at[0],
            device_id=(to_group, to_shard), device_id_type=MESH,
        ).start()

    each_device(send_token)
    for load in loads[3:]:
        load.start()
    tok_all[tile(s * groups + g), :] = tok_rows[tile(g), :]

    lane_block = lax.div(iota((1, lanes), 1), HEADS)
    lane_owner = jnp.full((1, lanes), -1, jnp.int32)
    lane_fill = jnp.zeros((1, lanes), jnp.int32)
    for b in range(blocks):
        lane_owner = jnp.where(lane_block == b, owner[b], lane_owner)
        lane_fill = jnp.where(lane_block == b, fill[b], lane_fill)
    pick = jnp.concatenate(
        [(iota((HEADS, rows), 1) == owner[b]).astype(f32) for b in range(blocks)]
        + [jnp.zeros((lanes - blocks * HEADS, rows), f32)], axis=0,
    ).astype(bf16)
    head_mask = lax.div(iota((HEADS, width), 1), head_dim) == iota((HEADS, width), 0)

    everyone = tok_all.at[pl.ds(0, (devices - 1) * chunks)]
    drain(everyone, recv_sem.at[0])
    x = jnp.concatenate(
        [tok_all[pl.ds(k, rows, stride=chunks), :] for k in range(chunks)], axis=1
    )
    normed = (
        x * lax.rsqrt(jnp.mean(x * x, axis=-1, keepdims=True) + epsilon) * attn_gain[...]
    ).astype(bf16)
    loads[0].wait()
    query = jnp.dot(normed, wq[...], preferred_element_type=f32).astype(bf16)

    spread = jnp.dot(pick, query, preferred_element_type=f32)
    query_heads = jnp.concatenate(
        [
            jnp.where(head_mask, spread[HEADS * b : HEADS * (b + 1)], 0.0)
            for b in range(lanes // HEADS)
        ], axis=0,
    ).astype(bf16)
    loads[1].wait()
    crossed = lax.dot_general(
        kc[...].reshape(blocks * span, width), query_heads,
        (((1,), (1,)), ((), ())), preferred_element_type=f32,
    )
    scores = jnp.zeros((span, lanes), f32)
    for b in range(blocks):
        scores = jnp.where(lane_block == b, crossed[span * b : span * (b + 1)], scores)
    valid = iota((span, lanes), 0) < lane_fill
    masked = jnp.where(valid, scores * scale, floor_score)
    block_max = jnp.max(masked, axis=0, keepdims=True)
    weights = jnp.where(valid, jnp.exp(masked - block_max), 0.0)
    weights = weights.astype(bf16).astype(f32)
    block_total = jnp.sum(weights, axis=0, keepdims=True)
    line = iota((8, 128), 0)
    stat = jnp.zeros((8, 128), f32)
    for i, value in enumerate((block_max, block_total, lane_owner.astype(f32))):
        stat = jnp.where(line == 2 * i, value[:, :128], stat)
        stat = jnp.where(line == 2 * i + 1, value[:, 128:], stat)
    stat_all[tile(s), :] = stat

    def send_stat(to_shard):
        pltpu.make_async_remote_copy(
            src_ref=stat_all.at[tile(s)], dst_ref=stat_all.at[tile(s)],
            send_sem=send_sem.at[1], recv_sem=recv_sem.at[1],
            device_id=(g, to_shard), device_id_type=MESH,
        ).start()

    each_shard(send_stat)

    stacked = jnp.concatenate(
        [jnp.where(lax.rem(lane_block, 4) == j, weights, 0.0) for j in range(4)], axis=0
    )
    stacked = jnp.transpose(stacked).astype(bf16)
    loads[2].wait()
    products = []
    for i in range(blocks // 4):
        product = jnp.dot(
            stacked[4 * HEADS * i : 4 * HEADS * (i + 1)],
            vc[4 * i : 4 * i + 4].reshape(4 * span, width), preferred_element_type=f32,
        )
        for j in range(4):
            products.append(jnp.where(head_mask, product[HEADS * j : HEADS * (j + 1)], 0.0))
    products.append(jnp.zeros((lanes - blocks * HEADS, width), f32))
    gather_heads = lax.div(iota((16, lanes), 1), HEADS) == iota((16, lanes), 0)
    block_sum = jnp.dot(
        gather_heads.astype(f32).astype(bf16), jnp.concatenate(products, axis=0).astype(bf16),
        preferred_element_type=f32,
    )
    for k in range(chunks):
        staged[pl.ds(k, blocks, stride=chunks), :] = block_sum[:blocks, 128 * k : 128 * (k + 1)]
    block_all[s] = staged[...].astype(bf16)

    def send_blocks(to_shard):
        pltpu.make_async_remote_copy(
            src_ref=block_all.at[s], dst_ref=block_all.at[s],
            send_sem=send_sem.at[2], recv_sem=recv_sem.at[2],
            device_id=(g, to_shard), device_id_type=MESH,
        ).start()

    each_shard(send_blocks)

    loads[3].wait()
    new = jnp.dot(normed, wkv[...], preferred_element_type=f32).astype(bf16).astype(f32)
    fold = lax.div(iota((width, lanes), 0), head_dim) == lax.rem(iota((width, lanes), 1), HEADS)
    own_score = (
        jnp.dot(
            query.astype(f32) * new[:, :width], fold.astype(f32),
            precision=lax.Precision.HIGHEST, preferred_element_type=f32,
        ) * scale
    )
    expand = lax.rem(iota((lanes, width), 0), HEADS) == lax.div(iota((lanes, width), 1), head_dim)
    expand = expand.astype(f32).astype(bf16)
    row_of = iota((padded, lanes), 0)
    shard_of = ((row_of.astype(f32) + 0.5) * (1.0 / blocks)).astype(jnp.int32)
    block_of = row_of - blocks * shard_of
    choose = ((shard_of[:, :shards] == iota((padded, shards), 1))).astype(f32)

    drain(stat_all.at[pl.ds(0, (shards - 1) * chunks)], recv_sem.at[1])
    maxima, sizes, owners = (
        jnp.concatenate(
            [stat_all[pl.ds(2 * i + j, shards, stride=chunks), :] for j in range(2)], axis=1
        )
        for i in range(3)
    )
    row_id = iota((rows, lanes), 0).astype(f32)
    members = [row_id == owners[i : i + 1] for i in range(shards)]
    peak = jnp.full((rows, lanes), floor_score, f32)
    for i in range(shards):
        peak = jnp.maximum(peak, jnp.where(members[i], maxima[i : i + 1], floor_score))
    for shift in (16, 32, 64, 128):
        peak = jnp.maximum(peak, pltpu.roll(peak, shift, 1))
    peak = jnp.maximum(peak, own_score)
    shard_id = iota((shards, lanes), 0)
    peaks = jnp.zeros((shards, lanes), f32)
    for i in range(shards):
        found = jnp.max(jnp.where(members[i], peak, floor_score), axis=0, keepdims=True)
        peaks = jnp.where(shard_id == i, found, peaks)
    factors = jnp.exp(maxima - peaks)
    sizes = sizes * factors
    totals = jnp.zeros((rows, lanes), f32)
    for i in range(shards):
        totals = totals + jnp.where(members[i], sizes[i : i + 1], 0.0)
    for shift in (16, 32, 64, 128):
        totals = totals + pltpu.roll(totals, shift, 1)
    own_gain = jnp.exp(own_score - peak)
    inverse = 1.0 / (totals + own_gain)
    own_gain = own_gain * inverse
    inverses = jnp.zeros((shards, lanes), f32)
    for i in range(shards):
        found = jnp.sum(jnp.where(members[i], inverse, 0.0), axis=0, keepdims=True)
        inverses = jnp.where(shard_id == i, found, inverses)
    spread_gain = jnp.dot(
        choose, factors * inverses,
        precision=lax.Precision.HIGHEST, preferred_element_type=f32,
    )
    spread_owner = jnp.dot(
        choose, owners, precision=lax.Precision.HIGHEST, preferred_element_type=f32
    )
    lane_id = iota((padded, lanes), 1)
    spread_gain = jnp.where(lax.div(lane_id, HEADS) == block_of, spread_gain, 0.0)
    gains = jnp.concatenate(
        [spread_gain, jnp.where(iota((rows, lanes), 1) < HEADS, own_gain, 0.0)], axis=0
    ).astype(bf16)
    gains = jnp.dot(gains, expand, preferred_element_type=f32)
    owner_of = jnp.sum(
        jnp.where(lane_id == HEADS * block_of, spread_owner, 0.0), axis=1, keepdims=True
    )
    wide = max(128, rows)
    owned = (iota((padded, wide), 1).astype(f32) == owner_of) & (iota((padded, wide), 0) < sums)
    owned = jnp.transpose(owned.astype(f32))[:rows].astype(bf16)
    own_part = new[:, width:] * gains[padded:]
    loads[4].wait()
    drain(block_all.at[pl.ds(0, shards - 1)], recv_sem.at[2])
    unpacked[...] = block_all[...].reshape(sums * chunks, 128).astype(f32)
    arrived = jnp.concatenate(
        [unpacked[pl.ds(k, sums, stride=chunks), :] for k in range(chunks)], axis=1
    )
    arrived = (arrived * gains[:sums]).astype(bf16)
    if padded > sums:
        arrived = jnp.concatenate([arrived, jnp.zeros((padded - sums, width), bf16)], axis=0)
    context = (jnp.dot(owned, arrived, preferred_element_type=f32) + own_part).astype(bf16)
    mixed = x + jnp.dot(context, wo[...], preferred_element_type=f32)
    mlp_rows = (
        mixed * lax.rsqrt(jnp.mean(mixed * mixed, axis=-1, keepdims=True) + epsilon)
        * mlp_gain[...]
    ).astype(bf16)
    loads[5].wait()
    loads[6].wait()
    gate = jnp.dot(mlp_rows, wgu[0], preferred_element_type=f32)
    up = jnp.dot(mlp_rows, wgu[1], preferred_element_type=f32)
    hidden = (gate / (1.0 + jnp.exp(-gate)) * up).astype(bf16)
    partial = jnp.dot(hidden, wd[...], preferred_element_type=f32)
    ours = lax.div(iota((rows, width), 0), groups) == s
    partial = partial + jnp.where(ours, mixed, 0.0)
    for k in range(chunks):
        down[pl.ds(k, rows, stride=chunks), :] = partial[:, 128 * k : 128 * (k + 1)]

    def send_down(to_group, to_shard):
        pltpu.make_async_remote_copy(
            src_ref=down.at[tile(to_shard * groups + to_group)],
            dst_ref=home.at[tile(g * shards + s)],
            send_sem=send_sem.at[3], recv_sem=recv_sem.at[3],
            device_id=(to_group, to_shard), device_id_type=MESH,
        ).start()

    each_device(send_down)
    home[tile(g * shards + s), :] = down[tile(s * groups + g), :]
    drain(everyone, send_sem.at[0])
    drain(stat_all.at[pl.ds(0, (shards - 1) * chunks)], send_sem.at[1])
    drain(block_all.at[pl.ds(0, shards - 1)], send_sem.at[2])
    drain(home.at[pl.ds(0, (devices - 1) * chunks)], recv_sem.at[3])
    for j in range(groups):
        row = home[j * shards * chunks : (j * shards + 1) * chunks, :]
        for i in range(1, shards):
            at = (j * shards + i) * chunks
            row = row + home[at : at + chunks, :]
        total[j * chunks : (j + 1) * chunks, :] = row
    out_ref[...] = jnp.concatenate(
        [total[pl.ds(k, groups, stride=chunks), :] for k in range(chunks)], axis=1
    )
    drain(home.at[pl.ds(0, (devices - 1) * chunks)], send_sem.at[3])


def body(
    tokens, attn_gain, w_qkv, w_out, mlp_gain, w_gate_up, w_down, kv_cache, block_owner, block_fill
):
    groups, shards = lax.axis_size("grp"), lax.axis_size("seq")
    row_count, width = tokens.shape
    blocks, _, span, _ = kv_cache.shape
    rows = groups * shards
    chunks = width // 128
    assert row_count == groups and chunks == 8 and groups == 4 and blocks % 4 == 0
    vmem = pl.BlockSpec(memory_space=pltpu.VMEM)
    smem = pl.BlockSpec(memory_space=pltpu.SMEM)
    hbm = pl.BlockSpec(memory_space=pl.ANY)
    output = pl.pallas_call(
        functools.partial(kernel, groups, shards),
        out_shape=jax.ShapeDtypeStruct((row_count, width), f32),
        in_specs=[vmem, vmem, hbm, hbm, vmem, hbm, hbm, hbm, smem, smem],
        out_specs=vmem,
        scratch_shapes=[
            pltpu.VMEM((width, width), bf16),
            pltpu.VMEM((width, 2 * width), bf16),
            pltpu.VMEM(w_out.shape, bf16),
            pltpu.VMEM(w_gate_up.shape, bf16),
            pltpu.VMEM(w_down.shape, bf16),
            pltpu.VMEM((blocks, span, width), bf16),
            pltpu.VMEM((blocks, span, width), bf16),
            pltpu.VMEM((row_count * chunks, 128), f32),
            pltpu.VMEM((rows * chunks, 128), f32),
            pltpu.VMEM((shards * chunks, 128), f32),
            pltpu.VMEM((blocks * chunks, 128), f32),
            pltpu.VMEM((shards, blocks * chunks, 128), bf16),
            pltpu.VMEM((shards * blocks * chunks, 128), f32),
            pltpu.VMEM((rows * chunks, 128), f32),
            pltpu.VMEM((rows * chunks, 128), f32),
            pltpu.VMEM((row_count * chunks, 128), f32),
            pltpu.SemaphoreType.DMA((7,)),
            pltpu.SemaphoreType.DMA((4,)),
            pltpu.SemaphoreType.DMA((4,)),
        ],
        compiler_params=pltpu.CompilerParams(
            collective_id=0, has_side_effects=True, vmem_limit_bytes=56 * 2**20
        ),
    )(
        tokens, attn_gain.reshape(1, width), w_qkv, w_out, mlp_gain.reshape(1, width),
        w_gate_up, w_down, kv_cache, block_owner, block_fill,
    )
    return output.astype(bf16)


def solution(mesh):
    in_specs = (
        P(("grp", "seq"), None),
        P(),
        P(),
        P(),
        P(),
        P(None, None, "seq"),
        P("seq", None),
        P(("grp", "seq"), None, None, None),
        P(("grp", "seq")),
        P(("grp", "seq")),
    )
    out_specs = P(("grp", "seq"), None)
    return jax.shard_map(body, mesh=mesh, in_specs=in_specs, out_specs=out_specs, check_vma=False)
```

time: 32.2 us -> 29.9 us (0.929)
  Pallas kernels: 30.6 us -> 28.3 us
    pallas_call x1, Pallas kernels: 30.6 us -> 28.3 us  [body(): pl.pallas_call(functools.partial(kernel, groups, shards), out_shape=jax.S...]
where the time goes in v2:
time: 29.9 us; the launch traced here: 29.7 us
  Pallas kernels  28.3 us (95%)
  other arithmetic  1.32 us (4%)
    pallas_call x1, Pallas kernels, body(): pl.pallas_call(functools.partial(kernel, groups, shards), out_shape=jax.S...  28.3 us
    convert_element_type x1, other arithmetic, body(): return output.astype(bf16)  1.32 us

profile of v2, /device:TPU:0, one launch (start us, length us, event | category | flops | bytes accessed | tf_op | source)
XLA Modules:
  0.0 29.7 jit_solution(2436793428613026265)
XLA Ops:
  0.0 28.3 %shard_map.100 = f32[4,1024]{1,0:T(4,128)} custom-call(bf16[4,1024]{1,0:T(4,128)(2,1)} %tokens.1, f32[1,1024]{1,0:T(1,128)} %bitcast.2, bf16[1024,3072]{1,0:T(8,128)(2,1)} %w_qkv.1, bf16[1024,1024]{1,0:T(8,128)(2,1)} %w_out.1, f32[1,1024]{1,0:T(1,128)} %bitcast.3, bf16[2,1024,512]{2,1,0:T(8,128)(2,1)} %w_gate_up.1, bf16[512,1024]{1,0:T(8,128)(2,1)} %w_down.1, ...), custom_call_target="tpu_custom_call" | custom-call | tf_op jit(solution)/shard_map/pallas_call | solution.py:338
  28.3 1.3 %convert_element_type.3 = bf16[4,1024]{1,0:T(4,128)(2,1)} convert(f32[4,1024]{1,0:T(4,128)} %shard_map.100) | non-fusion elementwise | flops 4096 | bytes 24576 | tf_op jit(solution)/shard_map/convert_element_type | solution.py:371

commit v3 on v2

--- a/solution.py
+++ b/solution.py
@@ -24,7 +24,7 @@
     tokens, attn_gain, w_qkv, w_out, mlp_gain, w_gate_up, w_down, kv_cache, owner, fill,
     out_ref,
     wq, wkv, wo, wgu, wd, kc, vc,
-    tok_rows, tok_all, stat_all, staged, block_all, unpacked, down, home, total,
+    tok_rows, tok_all, stat_all, staged, block_all, unpacked, wide_rows, down, home, total,
     load_sem, send_sem, recv_sem,
 ):
     g = lax.axis_index("grp")
@@ -55,6 +55,13 @@
     to_groups = [g] + [lax.rem(g + i, groups) for i in range(1, groups)]
 
     def each_device(act):
+        if shards <= 8:
+            for step in range(shards):
+                to_shard = lax.rem(s + step, shards)
+                for to_group in to_groups[0 if step else 1 :]:
+                    act(to_group, to_shard)
+            return
+
         def at(step, carry):
             to_shard = lax.rem(s + step, shards)
             for to_group in to_groups:
@@ -87,7 +94,8 @@
         load.start()
     mine = tokens[...].astype(f32)
     for k in range(chunks):
-        tok_rows[pl.ds(k, groups, stride=chunks), :] = mine[:, 128 * k : 128 * (k + 1)]
+        total[pl.ds(k, groups, stride=chunks), :] = mine[:, 128 * k : 128 * (k + 1)]
+    tok_rows[...] = total[...].reshape(groups, chunks, 128).astype(bf16)
     pl.semaphore_wait(barrier, devices - 1)
 
     def tile(index):
@@ -98,8 +106,8 @@
 
     def send_token(to_group, to_shard):
         pltpu.make_async_remote_copy(
-            src_ref=tok_rows.at[tile(to_group)],
-            dst_ref=tok_all.at[tile(s * groups + g)],
+            src_ref=tok_rows.at[to_group],
+            dst_ref=tok_all.at[s * groups + g],
             send_sem=send_sem.at[0], recv_sem=recv_sem.at[0],
             device_id=(to_group, to_shard), device_id_type=MESH,
         ).start()
@@ -107,7 +115,7 @@
     each_device(send_token)
     for load in loads[3:]:
         load.start()
-    tok_all[tile(s * groups + g), :] = tok_rows[tile(g), :]
+    tok_all[s * groups + g] = tok_rows[g]
 
     lane_block = lax.div(iota((1, lanes), 1), HEADS)
     lane_owner = jnp.full((1, lanes), -1, jnp.int32)
@@ -121,10 +129,11 @@
     ).astype(bf16)
     head_mask = lax.div(iota((HEADS, width), 1), head_dim) == iota((HEADS, width), 0)
 
-    everyone = tok_all.at[pl.ds(0, (devices - 1) * chunks)]
+    everyone = tok_all.at[pl.ds(0, devices - 1)]
     drain(everyone, recv_sem.at[0])
+    wide_rows[...] = tok_all[...].astype(f32).reshape(rows * chunks, 128)
     x = jnp.concatenate(
-        [tok_all[pl.ds(k, rows, stride=chunks), :] for k in range(chunks)], axis=1
+        [wide_rows[pl.ds(k, rows, stride=chunks), :] for k in range(chunks)], axis=1
     )
     normed = (
         x * lax.rsqrt(jnp.mean(x * x, axis=-1, keepdims=True) + epsilon) * attn_gain[...]
@@ -295,32 +304,32 @@
     ours = lax.div(iota((rows, width), 0), groups) == s
     partial = partial + jnp.where(ours, mixed, 0.0)
     for k in range(chunks):
-        down[pl.ds(k, rows, stride=chunks), :] = partial[:, 128 * k : 128 * (k + 1)]
+        wide_rows[pl.ds(k, rows, stride=chunks), :] = partial[:, 128 * k : 128 * (k + 1)]
+    down[...] = wide_rows[...].reshape(rows, chunks, 128).astype(bf16)
 
     def send_down(to_group, to_shard):
         pltpu.make_async_remote_copy(
-            src_ref=down.at[tile(to_shard * groups + to_group)],
-            dst_ref=home.at[tile(g * shards + s)],
+            src_ref=down.at[to_shard * groups + to_group],
+            dst_ref=home.at[g * shards + s],
             send_sem=send_sem.at[3], recv_sem=recv_sem.at[3],
             device_id=(to_group, to_shard), device_id_type=MESH,
         ).start()
 
     each_device(send_down)
-    home[tile(g * shards + s), :] = down[tile(s * groups + g), :]
+    home[g * shards + s] = down[s * groups + g]
     drain(everyone, send_sem.at[0])
     drain(stat_all.at[pl.ds(0, (shards - 1) * chunks)], send_sem.at[1])
     drain(block_all.at[pl.ds(0, shards - 1)], send_sem.at[2])
-    drain(home.at[pl.ds(0, (devices - 1) * chunks)], recv_sem.at[3])
+    drain(home.at[pl.ds(0, devices - 1)], recv_sem.at[3])
     for j in range(groups):
-        row = home[j * shards * chunks : (j * shards + 1) * chunks, :]
+        row = home[j * shards].astype(f32)
         for i in range(1, shards):
-            at = (j * shards + i) * chunks
-            row = row + home[at : at + chunks, :]
+            row = row + home[j * shards + i].astype(f32)
         total[j * chunks : (j + 1) * chunks, :] = row
     out_ref[...] = jnp.concatenate(
         [total[pl.ds(k, groups, stride=chunks), :] for k in range(chunks)], axis=1
     )
-    drain(home.at[pl.ds(0, (devices - 1) * chunks)], send_sem.at[3])
+    drain(home.at[pl.ds(0, devices - 1)], send_sem.at[3])
 
 
 def body(
@@ -348,14 +357,15 @@
             pltpu.VMEM(w_down.shape, bf16),
             pltpu.VMEM((blocks, span, width), bf16),
             pltpu.VMEM((blocks, span, width), bf16),
-            pltpu.VMEM((row_count * chunks, 128), f32),
-            pltpu.VMEM((rows * chunks, 128), f32),
+            pltpu.VMEM((row_count, chunks, 128), bf16),
+            pltpu.VMEM((rows, chunks, 128), bf16),
             pltpu.VMEM((shards * chunks, 128), f32),
             pltpu.VMEM((blocks * chunks, 128), f32),
             pltpu.VMEM((shards, blocks * chunks, 128), bf16),
             pltpu.VMEM((shards * blocks * chunks, 128), f32),
             pltpu.VMEM((rows * chunks, 128), f32),
-            pltpu.VMEM((rows * chunks, 128), f32),
+            pltpu.VMEM((rows, chunks, 128), bf16),
+            pltpu.VMEM((rows, chunks, 128), bf16),
             pltpu.VMEM((row_count * chunks, 128), f32),
             pltpu.SemaphoreType.DMA((7,)),
             pltpu.SemaphoreType.DMA((4,)),

time: 29.9 us -> 28.9 us (0.967)
  Pallas kernels: 28.3 us -> 27.3 us
    pallas_call x1, Pallas kernels: 28.3 us -> 27.3 us  [body(): pl.pallas_call(functools.partial(kernel, groups, shards), out_shape=jax.S...]
where the time goes in v3:
time: 28.9 us; the launch traced here: 28.7 us
  Pallas kernels  27.3 us (94%)
  other arithmetic  1.32 us (5%)
    pallas_call x1, Pallas kernels, body(): pl.pallas_call(functools.partial(kernel, groups, shards), out_shape=jax.S...  27.3 us
    convert_element_type x1, other arithmetic, body(): return output.astype(bf16)  1.32 us

profile of v3, /device:TPU:0, one launch (start us, length us, event | category | flops | bytes accessed | tf_op | source)
XLA Modules:
  0.0 28.7 jit_solution(8820924658582341078)
XLA Ops:
  0.0 27.3 %shard_map.100 = f32[4,1024]{1,0:T(4,128)} custom-call(bf16[4,1024]{1,0:T(4,128)(2,1)} %tokens.1, f32[1,1024]{1,0:T(1,128)} %bitcast.2, bf16[1024,3072]{1,0:T(8,128)(2,1)} %w_qkv.1, bf16[1024,1024]{1,0:T(8,128)(2,1)} %w_out.1, f32[1,1024]{1,0:T(1,128)} %bitcast.3, bf16[2,1024,512]{2,1,0:T(8,128)(2,1)} %w_gate_up.1, bf16[512,1024]{1,0:T(8,128)(2,1)} %w_down.1, ...), custom_call_target="tpu_custom_call" | custom-call | tf_op jit(solution)/shard_map/pallas_call | solution.py:347
  27.4 1.3 %convert_element_type.3 = bf16[4,1024]{1,0:T(4,128)(2,1)} convert(f32[4,1024]{1,0:T(4,128)} %shard_map.100) | non-fusion elementwise | flops 4096 | bytes 24576 | tf_op jit(solution)/shard_map/convert_element_type | solution.py:381
